TPU v7x, 32 devices: a whole 2x2x4 slice. The times are simulated.
32 devices in a mesh: grp: 2 (over x), slab: 16 (over z, y, core).
Axes of the slice: x: 2, y: 2, z: 4, core: 2. Of those that a mesh axis runs over, the one named last changes fastest.
Arguments:
- estimate: float32 [2, 8, 4, 48, 32], P(None, None, 'grp', 'slab'), parts along dimension 2, may hold values from -6 to 6
- measured: float32 [2, 8, 4, 48, 32], P(None, None, 'grp', 'slab'), parts along dimension 2, may hold values from -6 to 6
- sampled_lines: int32 [4, 12], P('grp'), parts along dimension 0, may hold values from 0 to 47, as said below
Outputs:
- updated: float32 [2, 8, 4, 48, 32], P(None, None, 'grp', 'slab'), parts along dimension 2
There are 2 independent parts, one for each index of `grp`. A program takes and returns all parts, laid end to end along the dimension named above; each array names one. Nothing has to cross between parts.
Inputs may be any that keep to these rules, and one draw needn't show every extreme that they name: `sampled_lines`: lines within a frame are distinct, and every frame contains line 48 // 2.
All inputs are finite; a program needn't handle non-finite values.
Results may differ from a plain program's by a relative error of at most 0.0001.
Values sent between devices are 32-bit elements; how exact they have to be, the bound alone decides.
No kernel may reach another device: no remote copies, remote signals or barrier semaphores. Data moves between devices by JAX's collectives and lax.ppermute only.
A program may use at most 64 MiB of HBM per device.

v0:
```python
import functools

import jax
import jax.numpy as jnp
from jax import lax
from jax.experimental import pallas as pl
from jax.experimental.pallas import tpu as pltpu
from jax.sharding import PartitionSpec as P

SPAN = 5
HALF = SPAN // 2
LAGS = SPAN - 1
LANES = 128
NT = (((1,), (1,)), ((), ()))
NN = (((1,), (0,)), ((), ()))


def up(size, unit):
    return -(-size // unit) * unit


def split(value):
    high = value.astype(jnp.bfloat16)
    return high, (value - high.astype(jnp.float32)).astype(jnp.bfloat16)


def repeat(count, body):
    if count <= 16:
        for step in range(count):
            body(step)
    else:
        lax.fori_loop(0, count, lambda step, carry: (body(step), carry)[1], 0)


def lane_tile(tile):
    start = tile * LANES
    return start if isinstance(start, int) else pl.multiple_of(start, LANES)


def kernel(sizes, hit_ref, gathered_ref, measured_ref, out_ref, x_ref, z_ref, zc_ref, acc_ref, xw_ref, lhs_ref, rhs_ref):
    slabs, coils, frames, rows, readout = sizes
    me = lax.axis_index("slab")
    cell = coils * frames
    band = SPAN * cell
    width = rows * readout
    groups = LANES // readout
    lines = slabs * rows
    tiles = up(lines, groups) // groups
    f32 = jnp.float32

    planes = 2 * frames

    def unpacked(block, plane, line):
        down, right = divmod(plane * rows + line, groups)
        return gathered_ref[block, down * coils : (down + 1) * coils, right * readout : (right + 1) * readout]

    if tiles * groups != lines:
        x_ref[...] = jnp.zeros_like(x_ref)
    for line in range(lines):
        block, inner = divmod(line, rows)
        group, tile = divmod(line, tiles)
        start = (LAGS + tile) * LANES + group * readout
        for plane in range(planes):
            x_ref[plane * coils : (plane + 1) * coils, start : start + readout] = unpacked(block, plane, inner)
    lane = lax.broadcasted_iota(jnp.int32, (2 * cell, LANES), 1)
    for back in range(1, LAGS + 1):
        source = (LAGS + tiles - back) * LANES
        wrapped = pltpu.roll(x_ref[:, source : source + LANES], readout, 1)
        target = (LAGS - back) * LANES
        x_ref[:, target : target + LANES] = jnp.where(lane >= readout, wrapped, 0.0)

    column = lane % readout
    inside = [(column + e - HALF >= 0) & (column + e - HALF < readout) for e in range(SPAN)]

    def patches(tile):
        at = pl.ds(lane_tile(tile), LANES)
        cells = x_ref[:, at]
        for e in range(SPAN):
            moved = cells if e == HALF else pltpu.roll(cells, (HALF - e) % LANES, 1)
            high, low = split(jnp.where(inside[e], moved, 0.0))
            for part in range(2):
                first = part * band + e * cell
                z_ref[first : first + cell, at] = high[part * cell : (part + 1) * cell]
                z_ref[2 * band + first : 2 * band + first + cell, at] = low[part * cell : (part + 1) * cell]

    repeat(LAGS + tiles, patches)

    pad = up(band, LANES)

    def centre(tile):
        source = pl.ds(lane_tile(tile + LAGS), LANES)
        at = pl.ds(lane_tile(tile), LANES)
        for piece in range(4):
            first = piece * pad
            zc_ref[first : first + band, at] = z_ref[piece * band : (piece + 1) * band, source]
            zc_ref[first + band : first + pad, at] = jnp.zeros((pad - band, LANES), jnp.bfloat16)

    repeat(tiles, centre)

    line_base = lane // readout * tiles
    acc_ref[...] = jnp.zeros_like(acc_ref)

    def energy(tile):
        cells = x_ref[:, pl.ds(lane_tile(tile + LAGS), LANES)]
        line = line_base + tile
        covers = jnp.minimum(line + HALF, lines - 1) - jnp.maximum(line - HALF, 0) + 1
        acc_ref[...] += cells * cells * covers.astype(f32)

    repeat(tiles, energy)
    row = lax.broadcasted_iota(jnp.int32, (2 * cell, LANES), 0)
    frame = row // coils % frames
    covers_t = jnp.minimum(frame + HALF, frames - 1) - jnp.maximum(frame - HALF, 0) + 1
    covers_x = jnp.minimum(column + HALF, readout - 1) - jnp.maximum(column - HALF, 0) + 1
    weighted = acc_ref[...] * (covers_t * covers_x).astype(f32)
    trace = jnp.sum(jnp.sum(weighted, axis=1, keepdims=True), axis=0, keepdims=True)
    scale = trace / (SPAN**3 * coils) + 1e-06

    def product(left, right):
        both = lax.dot_general(left, right[: 2 * pad], NT, preferred_element_type=f32)
        cross = lax.dot_general(left[: 2 * band], right[2 * pad :], NT, preferred_element_type=f32)
        return both[: 2 * band] + both[2 * band :] + cross

    mrow = lax.broadcasted_iota(jnp.int32, (band, pad), 0) // coils % frames
    mcol = lax.broadcasted_iota(jnp.int32, (band, pad), 1) // coils % frames
    mixes = []
    for shift in range(-frames + 1, frames):
        mask = jnp.zeros((band, pad), f32)
        for i in range(frames):
            for j in range(frames):
                if 0 <= i + shift < frames and 0 <= j + shift < frames:
                    count = sum(
                        abs(i - t) <= HALF and abs(j - t) <= HALF and 0 <= t + shift < frames for t in range(frames)
                    )
                    mask = jnp.where((mrow == i) & (mcol == j), float(count), mask)
        mixes.append((shift, mask))

    def mixed(gram):
        total = None
        for shift, mask in mixes:
            moved = gram
            if shift:
                moved = pltpu.roll(pltpu.roll(gram, -shift * coils % pad, 1), -shift * coils % band, 0)
            total = moved * mask if total is None else total + moved * mask
        return total

    def complex_gram(stacked):
        real = stacked[:band, :pad] + stacked[band:, pad:]
        imag = stacked[:band, pad:] - stacked[band:, :pad]
        return mixed(real), mixed(imag)

    slot = 0
    order = []

    def put(real, imag, lag, weight):
        nonlocal slot
        lhs_ref[:band, slot * pad : (slot + 1) * pad] = real
        lhs_ref[band:, slot * pad : (slot + 1) * pad] = imag
        order.append((lag, weight))
        slot += 1

    def put_both(pair, lag, weight, back_weight):
        real, imag = pair
        put(real, imag, lag, weight)
        fill = jnp.zeros((pad - band, pad), f32)
        real_t = jnp.transpose(jnp.concatenate([real, fill], axis=0))[:band]
        imag_t = jnp.transpose(jnp.concatenate([imag, fill], axis=0))[:band]
        put(real_t, -imag_t, -lag, back_weight)

    window = lax.broadcasted_iota(jnp.int32, (cell, up(width, LANES)), 1)
    my_line = me * rows + window // readout
    valid = [((my_line - b + HALF >= 0) & (my_line - b + HALF < lines)).astype(f32) for b in range(SPAN)]

    def lag_weight(lag):
        total = None
        for b in range(SPAN):
            if 0 <= b + lag < SPAN:
                total = valid[b] if total is None else total + valid[b]
        return total

    depth = max(d for d in range(1, 17) if tiles % d == 0)
    for lag in range(SPAN):

        def part(step):
            left = z_ref[:, pl.ds(lane_tile(LAGS - lag + step * depth), depth * LANES)]
            right = zc_ref[:, pl.ds(lane_tile(step * depth), depth * LANES)]
            return product(left, right)

        if tiles == depth:
            stacked = part(0)
        else:
            stacked = lax.fori_loop(
                0, tiles // depth, lambda step, total: total + part(step), jnp.zeros((2 * band, 2 * pad), f32)
            )
        pair = complex_gram(stacked)
        if lag == 0:
            put(*pair, 0, lag_weight(0))
        else:
            put_both(pair, lag, lag_weight(lag), lag_weight(-lag))

    def edge(first, second):
        group, tile = divmod(first, tiles)
        other = second % tiles
        start = (LAGS + tile) * LANES
        here = lax.broadcasted_iota(jnp.int32, (4 * band, LANES), 1) // readout == group
        left = jnp.where(here, z_ref[:, start : start + LANES].astype(f32), 0.0).astype(jnp.bfloat16)
        return complex_gram(product(left, zc_ref[:, other * LANES : (other + 1) * LANES]))

    last = lines - 1
    put(*edge(last - 1, last - 1), 0, -valid[0])
    put(*edge(last, last), 0, -(valid[0] + valid[1]))
    put(*edge(0, 0), 0, -(valid[3] + valid[4]))
    put(*edge(1, 1), 0, -valid[4])
    put_both(edge(last - 1, last), 1, -valid[0], -valid[1])
    put_both(edge(0, 1), 1, -valid[3], -valid[4])

    reach = up(LAGS, rows) // rows
    for j in range(-reach, reach + 1):
        block = me + j
        exists = (block >= 0) & (block < slabs)
        block = jnp.clip(block, 0, slabs - 1)
        for line in range(rows):
            start = (j + reach) * width + line * readout
            for plane in range(planes):
                held = jnp.where(exists, unpacked(block, plane, line), 0.0)
                xw_ref[plane * coils : (plane + 1) * coils, start : start + readout] = held
    extent = xw_ref.shape[1]
    spread = lax.broadcasted_iota(jnp.int32, (2 * cell, extent), 1) % readout
    around = xw_ref[...]
    wide = up(width, LANES)
    for e in range(SPAN):
        moved = around if e == HALF else pltpu.roll(around, (HALF - e) % extent, 1)
        near = spread + e - HALF
        moved = jnp.where((near >= 0) & (near < readout), moved, 0.0)
        for lag in range(-LAGS, LAGS + 1):
            start = (reach * rows + lag) * readout
            piece = moved[:, start : start + wide]
            for index, (at, weight) in enumerate(order):
                if at == lag:
                    first = index * pad + e * cell
                    for part in range(2):
                        high, low = split(piece[part * cell : (part + 1) * cell] * weight)
                        rhs_ref[first : first + cell, part * wide : (part + 1) * wide] = high
                        rhs_ref[first : first + cell, (2 + part) * wide : (3 + part) * wide] = low
    for index in range(len(order)):
        first = index * pad
        rhs_ref[first + band : first + pad, :] = jnp.zeros((pad - band, 4 * wide), jnp.bfloat16)

    high, low = split(lhs_ref[...])
    lead = rhs_ref[:, : 2 * wide]
    total = lax.dot_general(high, lead, NN, preferred_element_type=f32)
    total += lax.dot_general(low, lead, NN, preferred_element_type=f32)
    total += lax.dot_general(high, rhs_ref[:, 2 * wide :], NN, preferred_element_type=f32)
    real = total[:band, :wide] + total[band:, wide:]
    imag = total[:band, wide:] - total[band:, :wide]

    factor = 1.0 / (SPAN**3 * scale)
    column = window % readout
    for part, values in enumerate((real, imag)):
        folded = jnp.zeros((cell, wide), f32)
        for e in range(SPAN):
            moved = values[e * cell : (e + 1) * cell]
            if e != HALF:
                moved = pltpu.roll(moved, (e - HALF) % wide, 1)
            near = column - e + HALF
            folded += jnp.where((near >= 0) & (near < readout), moved, 0.0)
        folded = folded * factor
        for line in range(rows):
            for f in range(frames):
                kept = measured_ref[part, :, line, f, :]
                at = (slice(f * coils, (f + 1) * coils), slice(line * readout, (line + 1) * readout))
                out_ref[part, :, line, f, :] = jnp.where(hit_ref[at] > 0, kept, folded[at])


def pack(lines_ref, estimate_ref, packed_ref, hit_ref):
    _, coils, rows, frames, readout = estimate_ref.shape
    shape = hit_ref.shape
    line = lax.axis_index("slab") * rows + lax.broadcasted_iota(jnp.int32, shape, 1) // readout
    frame = lax.broadcasted_iota(jnp.int32, shape, 0) // coils
    hit = jnp.zeros(shape, jnp.int32)
    for f in range(frames):
        for sample in range(lines_ref.shape[1]):
            hit = jnp.where((line == lines_ref[f, sample]) & (frame == f), 1, hit)
    hit_ref[...] = hit
    groups = LANES // readout
    for part in range(2):
        for f in range(frames):
            for line in range(rows):
                down, right = divmod((part * frames + f) * rows + line, groups)
                at = (slice(down * coils, (down + 1) * coils), slice(right * readout, (right + 1) * readout))
                packed_ref[at] = estimate_ref[part, :, line, f, :]


def gather(block):
    copies = jnp.broadcast_to(block[None], (lax.axis_size("slab"),) + block.shape)
    return lax.all_to_all(copies, "slab", 0, 0)


def local(estimate, measured, sampled_lines):
    _, coils, frames, rows, readout = estimate.shape
    slabs = lax.axis_size("slab")
    cell = coils * frames
    width = rows * readout
    band = SPAN * cell
    pad = up(band, LANES)
    wide = up(width, LANES)
    groups = LANES // readout
    tiles = up(slabs * rows, groups) // groups
    reach = up(LAGS, rows) // rows
    slots = 2 * SPAN - 1 + 8

    vmem = pl.BlockSpec(memory_space=pltpu.VMEM)
    packed, hit = pl.pallas_call(
        pack,
        out_shape=(
            jax.ShapeDtypeStruct((up(2 * frames * rows, groups) // groups * coils, LANES), jnp.float32),
            jax.ShapeDtypeStruct((cell, wide), jnp.int32),
        ),
        in_specs=[pl.BlockSpec(memory_space=pltpu.SMEM), vmem],
        out_specs=(vmem, vmem),
        compiler_params=pltpu.CompilerParams(vmem_limit_bytes=2 * 1024 * 1024),
        name="pack",
    )(sampled_lines, jnp.swapaxes(estimate, 2, 3))
    gathered = gather(packed)
    sizes = (slabs, coils, frames, rows, readout)
    result = pl.pallas_call(
        functools.partial(kernel, sizes),
        out_shape=jax.ShapeDtypeStruct((2, coils, rows, frames, readout), jnp.float32),
        in_specs=[vmem, vmem, vmem],
        out_specs=vmem,
        scratch_shapes=[
            pltpu.VMEM((2 * cell, (LAGS + tiles) * LANES), jnp.float32),
            pltpu.VMEM((4 * band, (LAGS + tiles) * LANES), jnp.bfloat16),
            pltpu.VMEM((4 * pad, tiles * LANES), jnp.bfloat16),
            pltpu.VMEM((2 * cell, LANES), jnp.float32),
            pltpu.VMEM((2 * cell, up((2 * reach + 1) * width + LANES, LANES)), jnp.float32),
            pltpu.VMEM((2 * band, slots * pad), jnp.float32),
            pltpu.VMEM((slots * pad, 4 * wide), jnp.bfloat16),
        ],
        compiler_params=pltpu.CompilerParams(vmem_limit_bytes=40 * 1024 * 1024),
        name="filter_step",
    )(hit, gathered, jnp.swapaxes(measured, 2, 3))
    return jnp.swapaxes(result, 2, 3)


def solution(mesh):
    placed = (
        P(None, None, "grp", "slab", None),
        P(None, None, "grp", "slab", None),
        P("grp", None),
    )
    return jax.shard_map(
        local,
        mesh=mesh,
        in_specs=placed,
        out_specs=P(None, None, "grp", "slab", None),
        check_vma=False,
    )
```

profile of v0, /device:TPU:0, one launch (start us, length us, event | category | flops | bytes accessed | tf_op | source)
XLA Modules:
  0.0 24.7 jit_solution(15526858850417056045)
XLA Ops:
  0.0 0.0 copy-start.2
  0.0 0.7 %copy-done.2 = s32[2,12]{1,0:T(2,128)S(1)} copy-done((s32[2,12]{1,0:T(2,128)S(1)}, s32[2,12]{1,0:T(2,128)}, u32[]{:S(2)}) %copy-start.2) | copy-done | bytes 120
  0.7 0.0 copy-start.1
  0.7 0.8 %copy-done.1 = f32[2,8,2,3,32]{4,2,3,1,0:T(2,128)S(1)} copy-done((f32[2,8,2,3,32]{4,2,3,1,0:T(2,128)S(1)}, f32[2,8,2,3,32]{4,2,3,1,0:T(2,128)}, u32[]{:S(2)}) %copy-start.1) | copy-done | bytes 12312
  1.5 0.6 %pack.1 = (f32[24,128]{1,0:T(8,128)S(1)}, s32[16,128]{1,0:T(8,128)S(1)}) custom-call(s32[2,12]{1,0:T(2,128)S(1)} %copy-done.2, f32[2,8,3,2,32]{4,3,2,1,0:T(2,128)S(1)} %bitcast.4), custom_call_target="tpu_custom_call" | custom-call | tf_op jit(solution)/shard_map/pack/pallas_call | solution.py:312
  2.1 0.0 copy-start
  2.2 16.3 %all_to_all.5.gathered_ref = f32[16,24,128]{2,1,0:T(8,128)S(1)} all-to-all(f32[16,24,128]{2,1,0:T(8,128)S(1)} %broadcast_in_dim.2), channel_id=1, replica_groups=mesh['grp'=2,'slab'=16] {'slab'}, dimensions={0} | all-to-all | bytes 393216 | tf_op jit(solution)/shard_map/all_to_all | solution.py:295
  18.5 0.0 copy-done
  18.5 6.3 %filter_step.1 = f32[2,8,3,2,32]{4,3,2,1,0:T(2,128)} custom-call(s32[16,128]{1,0:T(8,128)S(1)} %get-tuple-element.7.hit_ref, f32[16,24,128]{2,1,0:T(8,128)S(1)} %all_to_all.5.gathered_ref, f32[2,8,3,2,32]{4,3,2,1,0:T(2,128)S(1)} %bitcast.3), custom_call_target="tpu_custom_call" | custom-call | tf_op jit(solution)/shard_map/filter_step/pallas_call | solution.py:325
  (1 shorter events, 0.0 us)
Async XLA Ops:
  0.0 0.7 %copy-start.2 = (s32[2,12]{1,0:T(2,128)S(1)}, s32[2,12]{1,0:T(2,128)}, u32[]{:S(2)}) copy-start(s32[2,12]{1,0:T(2,128)} %lines_ref.1) | copy-start | bytes 292
  0.7 0.8 %copy-start.1 = (f32[2,8,2,3,32]{4,2,3,1,0:T(2,128)S(1)}, f32[2,8,2,3,32]{4,2,3,1,0:T(2,128)}, u32[]{:S(2)}) copy-start(f32[2,8,2,3,32]{4,2,3,1,0:T(2,128)} %param.3) | copy-start | bytes 36868
  2.1 16.3 %copy-start = (f32[2,8,2,3,32]{4,2,3,1,0:T(2,128)S(1)}, f32[2,8,2,3,32]{4,2,3,1,0:T(2,128)}, u32[]{:S(2)}) copy-start(f32[2,8,2,3,32]{4,2,3,1,0:T(2,128)} %param.4) | copy-start | bytes 36868
where the time goes:
time: 25 us; the launch traced here: 24.7 us
  blocking collectives  16.3 us (65%)
  Pallas kernels  6.9 us (28%)
  local copies, waits for them, and re-layouts  1.5 us (6%)
    all_to_all x1, blocking collectives, gather(): return lax.all_to_all(copies, 'slab', 0, 0)  16.3 us
    pallas_call x1, Pallas kernels, local(): pl.pallas_call(functools.partial(kernel, sizes), out_shape=jax.ShapeDtype...  6.26 us
    unnamed x6, local copies, waits for them, and re-layouts  1.48 us
    pallas_call x1, Pallas kernels, local(): pl.pallas_call(pack, out_shape=(jax.ShapeDtypeStruct((up(2 * frames * row...  0.64 us

commit v1 on v0

--- a/solution.py
+++ b/solution.py
@@ -291,8 +291,7 @@
 
 
 def gather(block):
-    copies = jnp.broadcast_to(block[None], (lax.axis_size("slab"),) + block.shape)
-    return lax.all_to_all(copies, "slab", 0, 0)
+    return lax.all_gather(block, "slab")
 
 
 def local(estimate, measured, sampled_lines):
@@ -317,7 +316,7 @@
         ),
         in_specs=[pl.BlockSpec(memory_space=pltpu.SMEM), vmem],
         out_specs=(vmem, vmem),
-        compiler_params=pltpu.CompilerParams(vmem_limit_bytes=2 * 1024 * 1024),
+        compiler_params=pltpu.CompilerParams(vmem_limit_bytes=56 * 1024 * 1024),
         name="pack",
     )(sampled_lines, jnp.swapaxes(estimate, 2, 3))
     gathered = gather(packed)

time: 25 us -> 32 us (1.28)
  blocking collectives: 16.3 us -> 24 us
  local copies, waits for them, and re-layouts: 1.5 us -> 0.01 us
  Pallas kernels: 6.9 us -> 7.77 us
    all_gather x0 -> x1, blocking collectives: none -> 24 us  [gather(): return lax.all_gather(block, 'slab')]
    all_to_all x1 -> x0, blocking collectives: 16.3 us -> none  [gather(): return lax.all_to_all(copies, 'slab', 0, 0)]
    unnamed x6 -> x4, local copies, waits for them, and re-layouts: 1.48 us -> 0.01 us
    pallas_call x1, Pallas kernels: 0.64 us -> 1.5 us  [local(): pl.pallas_call(pack, out_shape=(jax.ShapeDtypeStruct((up(2 * frames * row...]
where the time goes in v1:
time: 32 us; the launch traced here: 31.8 us
  blocking collectives  24 us (75%)
  Pallas kernels  7.77 us (24%)
    all_gather x1, blocking collectives, gather(): return lax.all_gather(block, 'slab')  24 us
    pallas_call x1, Pallas kernels, local(): pl.pallas_call(functools.partial(kernel, sizes), out_shape=jax.ShapeDtype...  6.27 us
    pallas_call x1, Pallas kernels, local(): pl.pallas_call(pack, out_shape=(jax.ShapeDtypeStruct((up(2 * frames * row...  1.5 us

profile of v1, /device:TPU:0, one launch (start us, length us, event | category | flops | bytes accessed | tf_op | source)
XLA Modules:
  0.0 31.8 jit_solution(18438572730394541933)
XLA Ops:
  0.0 1.5 %pack.1 = (f32[24,128]{1,0:T(8,128)}, s32[16,128]{1,0:T(8,128)}) custom-call(s32[2,12]{1,0:T(2,128)} %lines_ref.1, f32[2,8,3,2,32]{4,3,2,1,0:T(2,128)} %bitcast.6), custom_call_target="tpu_custom_call" | custom-call | tf_op jit(solution)/shard_map/pack/pallas_call | solution.py:311
  1.5 0.0 copy-start
  1.5 0.0 copy-start.1
  1.5 24.0 %all-gather = f32[384,128]{1,0:T(8,128)S(1)} all-gather(f32[24,128]{1,0:T(8,128)} %get-tuple-element.8), channel_id=2, replica_groups=mesh['grp'=2,'slab'=16] {'slab'}, dimensions={0}, use_global_device_ids=true | all-gather | bytes 208896 | tf_op jit(solution)/shard_map/all_gather | solution.py:294
  25.5 0.0 copy-done
  25.5 0.0 copy-done.1
  25.5 6.3 %filter_step.1 = f32[2,8,3,2,32]{4,3,2,1,0:T(2,128)} custom-call(s32[16,128]{1,0:T(8,128)S(1)} %copy-done.1, f32[16,24,128]{2,1,0:T(8,128)S(1)} %bitcast.4, f32[2,8,3,2,32]{4,3,2,1,0:T(2,128)S(1)} %bitcast.5), custom_call_target="tpu_custom_call" | custom-call | tf_op jit(solution)/shard_map/filter_step/pallas_call | solution.py:324
Async XLA Ops:
  1.5 24.0 %copy-start = (f32[2,8,2,3,32]{4,2,3,1,0:T(2,128)S(1)}, f32[2,8,2,3,32]{4,2,3,1,0:T(2,128)}, u32[]{:S(2)}) copy-start(f32[2,8,2,3,32]{4,2,3,1,0:T(2,128)} %param.4) | copy-start | bytes 36868
  1.5 24.0 %copy-start.1 = (s32[16,128]{1,0:T(8,128)S(1)}, s32[16,128]{1,0:T(8,128)}, u32[]{:S(2)}) copy-start(s32[16,128]{1,0:T(8,128)} %get-tuple-element.7.hit_ref) | copy-start | bytes 24580

commit v2 on v1

--- a/solution.py
+++ b/solution.py
@@ -52,7 +52,7 @@
 
     def unpacked(block, plane, line):
         down, right = divmod(plane * rows + line, groups)
-        return gathered_ref[block, down * coils : (down + 1) * coils, right * readout : (right + 1) * readout]
+        return gathered_ref[place(block, slabs), down * coils : (down + 1) * coils, right * readout : (right + 1) * readout]
 
     if tiles * groups != lines:
         x_ref[...] = jnp.zeros_like(x_ref)
@@ -290,8 +290,31 @@
                 packed_ref[at] = estimate_ref[part, :, line, f, :]
 
 
+def steps(slabs):
+    stride, found = slabs, []
+    while stride > 1:
+        size = next(p for p in range(2, stride + 1) if stride % p == 0)
+        stride //= size
+        found.append((size, stride))
+    return found
+
+
+def place(block, slabs):
+    spot, weight = 0, 1
+    for size, stride in steps(slabs):
+        spot += block // stride % size * weight
+        weight *= size
+    return spot
+
+
 def gather(block):
-    return lax.all_gather(block, "slab")
+    slabs = lax.axis_size("slab")
+    held = block[None]
+    for size, stride in steps(slabs):
+        firsts = [i for i in range(slabs) if i // stride % size == 0]
+        groups = [[i + j * stride for j in range(size)] for i in firsts]
+        held = lax.all_gather(held, "slab", axis_index_groups=groups, tiled=True)
+    return held
 
 
 def local(estimate, measured, sampled_lines):

time: 32 us -> 26 us (0.81)
  blocking collectives: 24 us -> 18 us
    all_gather x1 -> x4, blocking collectives: 24 us -> 18 us  [gather(): held = lax.all_gather(held, 'slab', axis_index_groups=groups, tiled=True)]
where the time goes in v2:
time: 26 us; the launch traced here: 25.7 us
  blocking collectives  18 us (69%)
  Pallas kernels  7.76 us (30%)
    all_gather x4, blocking collectives, gather(): held = lax.all_gather(held, 'slab', axis_index_groups=groups, tiled=True)  18 us
    pallas_call x1, Pallas kernels, local(): pl.pallas_call(functools.partial(kernel, sizes), out_shape=jax.ShapeDtype...  6.26 us
    pallas_call x1, Pallas kernels, local(): pl.pallas_call(pack, out_shape=(jax.ShapeDtypeStruct((up(2 * frames * row...  1.5 us

profile of v2, /device:TPU:0, one launch (start us, length us, event | category | flops | bytes accessed | tf_op | source)
XLA Modules:
  0.0 25.7 jit_solution(1181760247518827040)
XLA Ops:
  0.0 1.5 %pack.1 = (f32[24,128]{1,0:T(8,128)}, s32[16,128]{1,0:T(8,128)}) custom-call(s32[2,12]{1,0:T(2,128)} %lines_ref.1, f32[2,8,3,2,32]{4,3,2,1,0:T(2,128)} %bitcast.6), custom_call_target="tpu_custom_call" | custom-call | tf_op jit(solution)/shard_map/pack/pallas_call | solution.py:334
  1.5 6.7 %all-gather = f32[48,128]{1,0:T(8,128)S(1)} all-gather(f32[24,128]{1,0:T(8,128)} %get-tuple-element.8), channel_id=2, replica_groups={{0,8},{1,9},{2,10},{3,11},{4,12},{5,13},{6,14},{7,15},{16,24},{17,25},{..., dimensions={0}, use_global_device_ids=true | all-gather | bytes 36864 | tf_op jit(solution)/shard_map/all_gather | solution.py:316
  8.2 4.5 %all_gather.13 = f32[4,24,128]{2,1,0:T(8,128)S(1)} all-gather(f32[2,24,128]{2,1,0:T(8,128)S(1)} %bitcast.5), channel_id=1, replica_groups={{0,4},{1,5},{2,6},{3,7},{8,12},{9,13},{10,14},{11,15},{16,20},{17,21},{..., dimensions={0}, use_global_device_ids=true | all-gather | bytes 73728 | tf_op jit(solution)/shard_map/all_gather | solution.py:316
  12.6 4.8 %all_gather.14 = f32[8,24,128]{2,1,0:T(8,128)S(1)} all-gather(f32[4,24,128]{2,1,0:T(8,128)S(1)} %all_gather.13), channel_id=1, replica_groups={{0,2},{1,3},{4,6},{5,7},{8,10},{9,11},{12,14},{13,15},{16,18},{17,19},{..., dimensions={0}, use_global_device_ids=true | all-gather | bytes 147456 | tf_op jit(solution)/shard_map/all_gather | solution.py:316
  17.4 0.0 copy-start
  17.4 0.0 copy-start.1
  17.4 2.1 %all_gather.15.gathered_ref = f32[16,24,128]{2,1,0:T(8,128)S(1)} all-gather(f32[8,24,128]{2,1,0:T(8,128)S(1)} %all_gather.14), channel_id=1, replica_groups={{0,1},{2,3},{4,5},{6,7},{8,9},{10,11},{12,13},{14,15},{16,17},{18,19},{..., dimensions={0}, use_global_device_ids=true | all-gather | bytes 294912 | tf_op jit(solution)/shard_map/all_gather | solution.py:316
  19.5 0.0 copy-done
  19.5 0.0 copy-done.1
  19.5 6.3 %filter_step.1 = f32[2,8,3,2,32]{4,3,2,1,0:T(2,128)} custom-call(s32[16,128]{1,0:T(8,128)S(1)} %copy-done.1, f32[16,24,128]{2,1,0:T(8,128)S(1)} %all_gather.15.gathered_ref, f32[2,8,3,2,32]{4,3,2,1,0:T(2,128)S(1)} %bitcast.4), custom_call_target="tpu_custom_call" | custom-call | tf_op jit(solution)/shard_map/filter_step/pallas_call | solution.py:347
Async XLA Ops:
  17.4 2.1 %copy-start = (f32[2,8,2,3,32]{4,2,3,1,0:T(2,128)S(1)}, f32[2,8,2,3,32]{4,2,3,1,0:T(2,128)}, u32[]{:S(2)}) copy-start(f32[2,8,2,3,32]{4,2,3,1,0:T(2,128)} %param.4) | copy-start | bytes 36868
  17.4 2.1 %copy-start.1 = (s32[16,128]{1,0:T(8,128)S(1)}, s32[16,128]{1,0:T(8,128)}, u32[]{:S(2)}) copy-start(s32[16,128]{1,0:T(8,128)} %get-tuple-element.7.hit_ref) | copy-start | bytes 24580

commit v3 on v1

--- a/solution.py
+++ b/solution.py
@@ -52,7 +52,7 @@
 
     def unpacked(block, plane, line):
         down, right = divmod(plane * rows + line, groups)
-        return gathered_ref[block, down * coils : (down + 1) * coils, right * readout : (right + 1) * readout]
+        return gathered_ref[place(block, slabs), down * coils : (down + 1) * coils, right * readout : (right + 1) * readout]
 
     if tiles * groups != lines:
         x_ref[...] = jnp.zeros_like(x_ref)
@@ -286,12 +286,28 @@
         for f in range(frames):
             for line in range(rows):
                 down, right = divmod((part * frames + f) * rows + line, groups)
-                at = (slice(down * coils, (down + 1) * coils), slice(right * readout, (right + 1) * readout))
+                at = (0, slice(down * coils, (down + 1) * coils), slice(right * readout, (right + 1) * readout))
                 packed_ref[at] = estimate_ref[part, :, line, f, :]
-
-
-def gather(block):
-    return lax.all_gather(block, "slab")
+    packed = packed_ref[0]
+    for copy in range(1, packed_ref.shape[0]):
+        packed_ref[copy] = packed
+
+
+def nearby(slabs):
+    return 2 if slabs % 2 == 0 else 1
+
+
+def place(block, slabs):
+    near = nearby(slabs)
+    return block % near * (slabs // near) + block // near
+
+
+def gather(copies, slabs):
+    near, far = nearby(slabs), slabs // nearby(slabs)
+    alike = [[i + j * near for j in range(far)] for i in range(near)]
+    chips = [[i * near + j for j in range(near)] for i in range(far)]
+    half = lax.all_to_all(copies, "slab", 0, 0, axis_index_groups=alike)
+    return lax.all_gather(half, "slab", axis_index_groups=chips, tiled=True)
 
 
 def local(estimate, measured, sampled_lines):
@@ -308,10 +324,11 @@
     slots = 2 * SPAN - 1 + 8
 
     vmem = pl.BlockSpec(memory_space=pltpu.VMEM)
+    copies = slabs // nearby(slabs)
     packed, hit = pl.pallas_call(
         pack,
         out_shape=(
-            jax.ShapeDtypeStruct((up(2 * frames * rows, groups) // groups * coils, LANES), jnp.float32),
+            jax.ShapeDtypeStruct((copies, up(2 * frames * rows, groups) // groups * coils, LANES), jnp.float32),
             jax.ShapeDtypeStruct((cell, wide), jnp.int32),
         ),
         in_specs=[pl.BlockSpec(memory_space=pltpu.SMEM), vmem],
@@ -319,7 +336,7 @@
         compiler_params=pltpu.CompilerParams(vmem_limit_bytes=56 * 1024 * 1024),
         name="pack",
     )(sampled_lines, jnp.swapaxes(estimate, 2, 3))
-    gathered = gather(packed)
+    gathered = gather(packed, slabs)
     sizes = (slabs, coils, frames, rows, readout)
     result = pl.pallas_call(
         functools.partial(kernel, sizes),

time: 32 us -> 24.6 us (0.77)
  blocking collectives: 24 us -> 16.5 us
    all_gather x1, blocking collectives: 24 us -> 2.07 us  [gather(): return lax.all_gather(half, 'slab', axis_index_groups=chips, tiled=True)]
    all_to_all x0 -> x1, blocking collectives: none -> 14.4 us  [gather(): half = lax.all_to_all(copies, 'slab', 0, 0, axis_index_groups=alike)]
where the time goes in v3:
time: 24.6 us; the launch traced here: 24.3 us
  blocking collectives  16.5 us (67%)
  Pallas kernels  7.8 us (32%)
    all_to_all x1, blocking collectives, gather(): half = lax.all_to_all(copies, 'slab', 0, 0, axis_index_groups=alike)  14.4 us
    pallas_call x1, Pallas kernels, local(): pl.pallas_call(functools.partial(kernel, sizes), out_shape=jax.ShapeDtype...  6.27 us
    all_gather x1, blocking collectives, gather(): return lax.all_gather(half, 'slab', axis_index_groups=chips, tiled=True)  2.07 us
    pallas_call x1, Pallas kernels, local(): pl.pallas_call(pack, out_shape=(jax.ShapeDtypeStruct((copies, up(2 * fram...  1.54 us

profile of v3, /device:TPU:0, one launch (start us, length us, event | category | flops | bytes accessed | tf_op | source)
XLA Modules:
  0.0 24.3 jit_solution(3713587284469009198)
XLA Ops:
  0.0 1.5 %pack.1 = (f32[8,24,128]{2,1,0:T(8,128)}, s32[16,128]{1,0:T(8,128)}) custom-call(s32[2,12]{1,0:T(2,128)} %lines_ref.1, f32[2,8,3,2,32]{4,3,2,1,0:T(2,128)} %bitcast.4), custom_call_target="tpu_custom_call" | custom-call | tf_op jit(solution)/shard_map/pack/pallas_call | solution.py:328
  1.5 14.4 %all_to_all.5 = f32[8,24,128]{2,1,0:T(8,128)S(1)} all-to-all(f32[8,24,128]{2,1,0:T(8,128)} %get-tuple-element.8), channel_id=1, replica_groups={{0,2,4,6,8,10,12,14},{1,3,5,7,9,11,13,15},{16,18,20,22,24,26,28,30},{17..., dimensions={0} | all-to-all | bytes 196608 | tf_op jit(solution)/shard_map/all_to_all | solution.py:309
  15.9 0.0 copy-start
  15.9 0.0 copy-start.1
  15.9 2.1 %all_gather.3.gathered_ref = f32[16,24,128]{2,1,0:T(8,128)S(1)} all-gather(f32[8,24,128]{2,1,0:T(8,128)S(1)} %all_to_all.5), channel_id=1, replica_groups={{0,1},{2,3},{4,5},{6,7},{8,9},{10,11},{12,13},{14,15},{16,17},{18,19},{..., dimensions={0}, use_global_device_ids=true | all-gather | bytes 294912 | tf_op jit(solution)/shard_map/all_gather | solution.py:310
  18.0 0.0 copy-done
  18.0 0.0 copy-done.1
  18.0 6.3 %filter_step.1 = f32[2,8,3,2,32]{4,3,2,1,0:T(2,128)} custom-call(s32[16,128]{1,0:T(8,128)S(1)} %copy-done.1, f32[16,24,128]{2,1,0:T(8,128)S(1)} %all_gather.3.gathered_ref, f32[2,8,3,2,32]{4,3,2,1,0:T(2,128)S(1)} %bitcast.3), custom_call_target="tpu_custom_call" | custom-call | tf_op jit(solution)/shard_map/filter_step/pallas_call | solution.py:341
Async XLA Ops:
  15.9 2.1 %copy-start = (f32[2,8,2,3,32]{4,2,3,1,0:T(2,128)S(1)}, f32[2,8,2,3,32]{4,2,3,1,0:T(2,128)}, u32[]{:S(2)}) copy-start(f32[2,8,2,3,32]{4,2,3,1,0:T(2,128)} %param.4) | copy-start | bytes 36868
  15.9 2.1 %copy-start.1 = (s32[16,128]{1,0:T(8,128)S(1)}, s32[16,128]{1,0:T(8,128)}, u32[]{:S(2)}) copy-start(s32[16,128]{1,0:T(8,128)} %get-tuple-element.7.hit_ref) | copy-start | bytes 24580

commit v4 on v1

--- a/solution.py
+++ b/solution.py
@@ -42,6 +42,7 @@
     me = lax.axis_index("slab")
     cell = coils * frames
     band = SPAN * cell
+    pad = up(band, LANES)
     width = rows * readout
     groups = LANES // readout
     lines = slabs * rows
@@ -72,27 +73,47 @@
     column = lane % readout
     inside = [(column + e - HALF >= 0) & (column + e - HALF < readout) for e in range(SPAN)]
 
+    stacked = stacks(tiles)
+    held = SPAN if stacked else 1
+
     def patches(tile):
-        at = pl.ds(lane_tile(tile), LANES)
-        cells = x_ref[:, at]
+        source = pl.ds(lane_tile(tile), LANES)
+        if stacked:
+            targets = [(lag, tile - LAGS + lag) for lag in range(SPAN) if 0 <= tile - LAGS + lag < tiles]
+        else:
+            targets = [(0, tile)]
+        cells = x_ref[:, source]
         for e in range(SPAN):
             moved = cells if e == HALF else pltpu.roll(cells, (HALF - e) % LANES, 1)
             high, low = split(jnp.where(inside[e], moved, 0.0))
-            for part in range(2):
-                first = part * band + e * cell
-                z_ref[first : first + cell, at] = high[part * cell : (part + 1) * cell]
-                z_ref[2 * band + first : 2 * band + first + cell, at] = low[part * cell : (part + 1) * cell]
-
-    repeat(LAGS + tiles, patches)
-
-    pad = up(band, LANES)
+            for lag, target in targets:
+                at = pl.ds(lane_tile(target), LANES)
+                for part in range(2):
+                    first = (2 * lag + part) * band + e * cell
+                    z_ref[first : first + cell, at] = high[part * cell : (part + 1) * cell]
+                    first += 2 * held * band
+                    z_ref[first : first + cell, at] = low[part * cell : (part + 1) * cell]
+            if stacked and tile >= LAGS:
+                at = pl.ds(lane_tile(tile - LAGS), LANES)
+                for part in range(2):
+                    first = part * pad + e * cell
+                    zc_ref[first : first + cell, at] = high[part * cell : (part + 1) * cell]
+                    first += 2 * pad
+                    zc_ref[first : first + cell, at] = low[part * cell : (part + 1) * cell]
+
+    if stacked:
+        for tile in range(LAGS + tiles):
+            patches(tile)
+    else:
+        repeat(LAGS + tiles, patches)
 
     def centre(tile):
         source = pl.ds(lane_tile(tile + LAGS), LANES)
         at = pl.ds(lane_tile(tile), LANES)
         for piece in range(4):
             first = piece * pad
-            zc_ref[first : first + band, at] = z_ref[piece * band : (piece + 1) * band, source]
+            if not stacked:
+                zc_ref[first : first + band, at] = z_ref[piece * band : (piece + 1) * band, source]
             zc_ref[first + band : first + pad, at] = jnp.zeros((pad - band, LANES), jnp.bfloat16)
 
     repeat(tiles, centre)
@@ -116,9 +137,10 @@
     scale = trace / (SPAN**3 * coils) + 1e-06
 
     def product(left, right):
+        half = left.shape[0] // 2
         both = lax.dot_general(left, right[: 2 * pad], NT, preferred_element_type=f32)
-        cross = lax.dot_general(left[: 2 * band], right[2 * pad :], NT, preferred_element_type=f32)
-        return both[: 2 * band] + both[2 * band :] + cross
+        cross = lax.dot_general(left[:half], right[2 * pad :], NT, preferred_element_type=f32)
+        return both[:half] + both[half:] + cross
 
     mrow = lax.broadcasted_iota(jnp.int32, (band, pad), 0) // coils % frames
     mcol = lax.broadcasted_iota(jnp.int32, (band, pad), 1) // coils % frames
@@ -143,9 +165,9 @@
             total = moved * mask if total is None else total + moved * mask
         return total
 
-    def complex_gram(stacked):
-        real = stacked[:band, :pad] + stacked[band:, pad:]
-        imag = stacked[:band, pad:] - stacked[band:, :pad]
+    def complex_gram(sums):
+        real = sums[:band, :pad] + sums[band:, pad:]
+        imag = sums[:band, pad:] - sums[band:, :pad]
         return mixed(real), mixed(imag)
 
     slot = 0
@@ -177,6 +199,8 @@
                 total = valid[b] if total is None else total + valid[b]
         return total
 
+    if stacked:
+        every = product(z_ref[...], zc_ref[...])
     depth = max(d for d in range(1, 17) if tiles % d == 0)
     for lag in range(SPAN):
 
@@ -185,13 +209,13 @@
             right = zc_ref[:, pl.ds(lane_tile(step * depth), depth * LANES)]
             return product(left, right)
 
-        if tiles == depth:
-            stacked = part(0)
+        if stacked:
+            sums = every[2 * band * lag : 2 * band * (lag + 1)]
         else:
-            stacked = lax.fori_loop(
+            sums = lax.fori_loop(
                 0, tiles // depth, lambda step, total: total + part(step), jnp.zeros((2 * band, 2 * pad), f32)
             )
-        pair = complex_gram(stacked)
+        pair = complex_gram(sums)
         if lag == 0:
             put(*pair, 0, lag_weight(0))
         else:
@@ -200,9 +224,13 @@
     def edge(first, second):
         group, tile = divmod(first, tiles)
         other = second % tiles
-        start = (LAGS + tile) * LANES
-        here = lax.broadcasted_iota(jnp.int32, (4 * band, LANES), 1) // readout == group
-        left = jnp.where(here, z_ref[:, start : start + LANES].astype(f32), 0.0).astype(jnp.bfloat16)
+        start = tile * LANES if stacked else (LAGS + tile) * LANES
+        here = lax.broadcasted_iota(jnp.int32, (2 * band, LANES), 1) // readout == group
+        halves = []
+        for base in (0, 2 * held * band):
+            value = z_ref[base : base + 2 * band, start : start + LANES].astype(f32)
+            halves.append(jnp.where(here, value, 0.0).astype(jnp.bfloat16))
+        left = jnp.concatenate(halves, axis=0)
         return complex_gram(product(left, zc_ref[:, other * LANES : (other + 1) * LANES]))
 
     last = lines - 1
@@ -286,12 +314,19 @@
         for f in range(frames):
             for line in range(rows):
                 down, right = divmod((part * frames + f) * rows + line, groups)
-                at = (slice(down * coils, (down + 1) * coils), slice(right * readout, (right + 1) * readout))
+                at = (0, slice(down * coils, (down + 1) * coils), slice(right * readout, (right + 1) * readout))
                 packed_ref[at] = estimate_ref[part, :, line, f, :]
-
-
-def gather(block):
-    return lax.all_gather(block, "slab")
+    packed = packed_ref[0]
+    for copy in range(1, packed_ref.shape[0]):
+        packed_ref[copy] = packed
+
+
+def gather(copies):
+    return lax.all_to_all(copies, "slab", 0, 0)
+
+
+def stacks(tiles):
+    return tiles <= 16
 
 
 def local(estimate, measured, sampled_lines):
@@ -306,12 +341,13 @@
     tiles = up(slabs * rows, groups) // groups
     reach = up(LAGS, rows) // rows
     slots = 2 * SPAN - 1 + 8
+    columns = (tiles if stacks(tiles) else LAGS + tiles) * LANES
 
     vmem = pl.BlockSpec(memory_space=pltpu.VMEM)
     packed, hit = pl.pallas_call(
         pack,
         out_shape=(
-            jax.ShapeDtypeStruct((up(2 * frames * rows, groups) // groups * coils, LANES), jnp.float32),
+            jax.ShapeDtypeStruct((slabs, up(2 * frames * rows, groups) // groups * coils, LANES), jnp.float32),
             jax.ShapeDtypeStruct((cell, wide), jnp.int32),
         ),
         in_specs=[pl.BlockSpec(memory_space=pltpu.SMEM), vmem],
@@ -328,7 +364,7 @@
         out_specs=vmem,
         scratch_shapes=[
             pltpu.VMEM((2 * cell, (LAGS + tiles) * LANES), jnp.float32),
-            pltpu.VMEM((4 * band, (LAGS + tiles) * LANES), jnp.bfloat16),
+            pltpu.VMEM((4 * band * (SPAN if stacks(tiles) else 1), columns), jnp.bfloat16),
             pltpu.VMEM((4 * pad, tiles * LANES), jnp.bfloat16),
             pltpu.VMEM((2 * cell, LANES), jnp.float32),
             pltpu.VMEM((2 * cell, up((2 * reach + 1) * width + LANES, LANES)), jnp.float32),

time: 32 us -> 24.3 us (0.76)
  blocking collectives: 24 us -> 16.5 us
    all_gather x1 -> x0, blocking collectives: 24 us -> none  [gather(): return lax.all_gather(block, 'slab')]
    all_to_all x0 -> x1, blocking collectives: none -> 16.5 us  [gather(): return lax.all_to_all(copies, 'slab', 0, 0)]
    pallas_call x1, Pallas kernels: 6.27 us -> 5.9 us  [local(): pl.pallas_call(functools.partial(kernel, sizes), out_shape=jax.ShapeDtype...]
where the time goes in v4:
time: 24.3 us; the launch traced here: 24 us
  blocking collectives  16.5 us (68%)
  Pallas kernels  7.48 us (31%)
    all_to_all x1, blocking collectives, gather(): return lax.all_to_all(copies, 'slab', 0, 0)  16.5 us
    pallas_call x1, Pallas kernels, local(): pl.pallas_call(functools.partial(kernel, sizes), out_shape=jax.ShapeDtype...  5.9 us
    pallas_call x1, Pallas kernels, local(): pl.pallas_call(pack, out_shape=(jax.ShapeDtypeStruct((slabs, up(2 * frame...  1.58 us

profile of v4, /device:TPU:0, one launch (start us, length us, event | category | flops | bytes accessed | tf_op | source)
XLA Modules:
  0.0 24.0 jit_solution(7316801396899077944)
XLA Ops:
  0.0 1.6 %pack.1 = (f32[16,24,128]{2,1,0:T(8,128)}, s32[16,128]{1,0:T(8,128)}) custom-call(s32[2,12]{1,0:T(2,128)} %lines_ref.1, f32[2,8,3,2,32]{4,3,2,1,0:T(2,128)} %bitcast.4), custom_call_target="tpu_custom_call" | custom-call | tf_op jit(solution)/shard_map/pack/pallas_call | solution.py:347
  1.6 0.0 copy-start
  1.6 0.0 copy-start.1
  1.6 16.5 %all_to_all.5.gathered_ref = f32[16,24,128]{2,1,0:T(8,128)S(1)} all-to-all(f32[16,24,128]{2,1,0:T(8,128)} %get-tuple-element.8), channel_id=1, replica_groups=mesh['grp'=2,'slab'=16] {'slab'}, dimensions={0} | all-to-all | bytes 393216 | tf_op jit(solution)/shard_map/all_to_all | solution.py:325
  18.1 0.0 copy-done
  18.1 0.0 copy-done.1
  18.1 5.9 %filter_step.1 = f32[2,8,3,2,32]{4,3,2,1,0:T(2,128)} custom-call(s32[16,128]{1,0:T(8,128)S(1)} %copy-done.1, f32[16,24,128]{2,1,0:T(8,128)S(1)} %all_to_all.5.gathered_ref, f32[2,8,3,2,32]{4,3,2,1,0:T(2,128)S(1)} %bitcast.3), custom_call_target="tpu_custom_call" | custom-call | tf_op jit(solution)/shard_map/filter_step/pallas_call | solution.py:360
Async XLA Ops:
  1.6 16.5 %copy-start = (f32[2,8,2,3,32]{4,2,3,1,0:T(2,128)S(1)}, f32[2,8,2,3,32]{4,2,3,1,0:T(2,128)}, u32[]{:S(2)}) copy-start(f32[2,8,2,3,32]{4,2,3,1,0:T(2,128)} %param.4) | copy-start | bytes 36868
  1.6 16.5 %copy-start.1 = (s32[16,128]{1,0:T(8,128)S(1)}, s32[16,128]{1,0:T(8,128)}, u32[]{:S(2)}) copy-start(s32[16,128]{1,0:T(8,128)} %get-tuple-element.7.hit_ref) | copy-start | bytes 24580

commit v5 on v4

v5 whole, which is shorter than its diff:
```python
import functools

import jax
import jax.numpy as jnp
from jax import lax
from jax.experimental import pallas as pl
from jax.experimental.pallas import tpu as pltpu
from jax.sharding import PartitionSpec as P

SPAN = 5
HALF = SPAN // 2
LAGS = SPAN - 1
LANES = 128
NT = (((1,), (1,)), ((), ()))
NN = (((1,), (0,)), ((), ()))


def up(size, unit):
    return -(-size // unit) * unit


def split(value):
    high = value.astype(jnp.bfloat16)
    return high, (value - high.astype(jnp.float32)).astype(jnp.bfloat16)


def repeat(count, body):
    if count <= 16:
        for step in range(count):
            body(step)
    else:
        lax.fori_loop(0, count, lambda step, carry: (body(step), carry)[1], 0)


def lane_tile(tile):
    start = tile * LANES
    return start if isinstance(start, int) else pl.multiple_of(start, LANES)


def kernel(sizes, hit_ref, gathered_ref, measured_ref, out_ref, x_ref, z_ref, zc_ref, acc_ref, xw_ref, lhs_ref, rhs_ref):
    slabs, coils, frames, rows, readout = sizes
    me = lax.axis_index("slab")
    cell = coils * frames
    band = SPAN * cell
    pad = up(band, LANES)
    width = rows * readout
    groups = LANES // readout
    lines = slabs * rows
    tiles = up(lines, groups) // groups
    f32 = jnp.float32

    planes = 2 * frames

    def unpacked(block, plane, line):
        down, right = divmod(plane * rows + line, groups)
        return gathered_ref[block, down * coils : (down + 1) * coils, right * readout : (right + 1) * readout]

    window = lax.broadcasted_iota(jnp.int32, (cell, up(width, LANES)), 1)
    my_line = me * rows + window // readout
    valid = [((my_line - b + HALF >= 0) & (my_line - b + HALF < lines)).astype(f32) for b in range(SPAN)]

    def lag_weight(lag):
        total = None
        for b in range(SPAN):
            if 0 <= b + lag < SPAN:
                total = valid[b] if total is None else total + valid[b]
        return total

    order = [(0, lag_weight(0))]
    for lag in range(1, SPAN):
        order += [(lag, lag_weight(lag)), (-lag, lag_weight(-lag))]
    order += [(0, -valid[0]), (0, -(valid[0] + valid[1])), (0, -(valid[3] + valid[4])), (0, -valid[4])]
    order += [(1, -valid[0]), (-1, -valid[1]), (1, -valid[3]), (-1, -valid[4])]

    reach = up(LAGS, rows) // rows
    for j in range(-reach, reach + 1):
        block = me + j
        exists = (block >= 0) & (block < slabs)
        block = jnp.clip(block, 0, slabs - 1)
        for line in range(rows):
            start = (j + reach) * width + line * readout
            for plane in range(planes):
                held = jnp.where(exists, unpacked(block, plane, line), 0.0)
                xw_ref[plane * coils : (plane + 1) * coils, start : start + readout] = held
    extent = xw_ref.shape[1]
    spread = lax.broadcasted_iota(jnp.int32, (2 * cell, extent), 1) % readout
    around = xw_ref[...]
    wide = up(width, LANES)
    for e in range(SPAN):
        moved = around if e == HALF else pltpu.roll(around, (HALF - e) % extent, 1)
        near = spread + e - HALF
        moved = jnp.where((near >= 0) & (near < readout), moved, 0.0)
        for lag in range(-LAGS, LAGS + 1):
            start = (reach * rows + lag) * readout
            piece = moved[:, start : start + wide]
            for index, (at, weight) in enumerate(order):
                if at == lag:
                    first = index * pad + e * cell
                    for part in range(2):
                        high, low = split(piece[part * cell : (part + 1) * cell] * weight)
                        rhs_ref[first : first + cell, part * wide : (part + 1) * wide] = high
                        rhs_ref[first : first + cell, (2 + part) * wide : (3 + part) * wide] = low
    for index in range(len(order)):
        first = index * pad
        rhs_ref[first + band : first + pad, :] = jnp.zeros((pad - band, 4 * wide), jnp.bfloat16)

    if tiles * groups != lines:
        x_ref[...] = jnp.zeros_like(x_ref)
    for line in range(lines):
        block, inner = divmod(line, rows)
        group, tile = divmod(line, tiles)
        start = (LAGS + tile) * LANES + group * readout
        for plane in range(planes):
            x_ref[plane * coils : (plane + 1) * coils, start : start + readout] = unpacked(block, plane, inner)
    lane = lax.broadcasted_iota(jnp.int32, (2 * cell, LANES), 1)
    for back in range(1, LAGS + 1):
        source = (LAGS + tiles - back) * LANES
        wrapped = pltpu.roll(x_ref[:, source : source + LANES], readout, 1)
        target = (LAGS - back) * LANES
        x_ref[:, target : target + LANES] = jnp.where(lane >= readout, wrapped, 0.0)

    column = lane % readout
    inside = [(column + e - HALF >= 0) & (column + e - HALF < readout) for e in range(SPAN)]

    stacked = stacks(tiles)
    held = SPAN if stacked else 1

    def patches(tile):
        source = pl.ds(lane_tile(tile), LANES)
        if stacked:
            targets = [(lag, tile - LAGS + lag) for lag in range(SPAN) if 0 <= tile - LAGS + lag < tiles]
        else:
            targets = [(0, tile)]
        cells = x_ref[:, source]
        for e in range(SPAN):
            moved = cells if e == HALF else pltpu.roll(cells, (HALF - e) % LANES, 1)
            high, low = split(jnp.where(inside[e], moved, 0.0))
            for lag, target in targets:
                at = pl.ds(lane_tile(target), LANES)
                for part in range(2):
                    first = (2 * lag + part) * band + e * cell
                    z_ref[first : first + cell, at] = high[part * cell : (part + 1) * cell]
                    first += 2 * held * band
                    z_ref[first : first + cell, at] = low[part * cell : (part + 1) * cell]
            if stacked and tile >= LAGS:
                at = pl.ds(lane_tile(tile - LAGS), LANES)
                for part in range(2):
                    first = part * pad + e * cell
                    zc_ref[first : first + cell, at] = high[part * cell : (part + 1) * cell]
                    first += 2 * pad
                    zc_ref[first : first + cell, at] = low[part * cell : (part + 1) * cell]

    if stacked:
        for tile in range(LAGS + tiles):
            patches(tile)
    else:
        repeat(LAGS + tiles, patches)

    def centre(tile):
        source = pl.ds(lane_tile(tile + LAGS), LANES)
        at = pl.ds(lane_tile(tile), LANES)
        for piece in range(4):
            first = piece * pad
            if not stacked:
                zc_ref[first : first + band, at] = z_ref[piece * band : (piece + 1) * band, source]
            zc_ref[first + band : first + pad, at] = jnp.zeros((pad - band, LANES), jnp.bfloat16)

    repeat(tiles, centre)

    line_base = lane // readout * tiles
    acc_ref[...] = jnp.zeros_like(acc_ref)

    def energy(tile):
        cells = x_ref[:, pl.ds(lane_tile(tile + LAGS), LANES)]
        line = line_base + tile
        covers = jnp.minimum(line + HALF, lines - 1) - jnp.maximum(line - HALF, 0) + 1
        acc_ref[...] += cells * cells * covers.astype(f32)

    repeat(tiles, energy)
    row = lax.broadcasted_iota(jnp.int32, (2 * cell, LANES), 0)
    frame = row // coils % frames
    covers_t = jnp.minimum(frame + HALF, frames - 1) - jnp.maximum(frame - HALF, 0) + 1
    covers_x = jnp.minimum(column + HALF, readout - 1) - jnp.maximum(column - HALF, 0) + 1
    weighted = acc_ref[...] * (covers_t * covers_x).astype(f32)
    trace = jnp.sum(jnp.sum(weighted, axis=1, keepdims=True), axis=0, keepdims=True)
    scale = trace / (SPAN**3 * coils) + 1e-06

    def product(left, right):
        half = left.shape[0] // 2
        both = lax.dot_general(left, right[: 2 * pad], NT, preferred_element_type=f32)
        cross = lax.dot_general(left[:half], right[2 * pad :], NT, preferred_element_type=f32)
        return both[:half] + both[half:] + cross

    mrow = lax.broadcasted_iota(jnp.int32, (band, pad), 0) // coils % frames
    mcol = lax.broadcasted_iota(jnp.int32, (band, pad), 1) // coils % frames
    mixes = []
    for shift in range(-frames + 1, frames):
        mask = jnp.zeros((band, pad), f32)
        for i in range(frames):
            for j in range(frames):
                if 0 <= i + shift < frames and 0 <= j + shift < frames:
                    count = sum(
                        abs(i - t) <= HALF and abs(j - t) <= HALF and 0 <= t + shift < frames for t in range(frames)
                    )
                    mask = jnp.where((mrow == i) & (mcol == j), float(count), mask)
        mixes.append((shift, mask))

    def mixed(gram):
        total = None
        for shift, mask in mixes:
            moved = gram
            if shift:
                moved = pltpu.roll(pltpu.roll(gram, -shift * coils % pad, 1), -shift * coils % band, 0)
            total = moved * mask if total is None else total + moved * mask
        return total

    def complex_gram(sums):
        real = sums[:band, :pad] + sums[band:, pad:]
        imag = sums[:band, pad:] - sums[band:, :pad]
        return mixed(real), mixed(imag)

    slot = 0

    def put(real, imag):
        nonlocal slot
        lhs_ref[:band, slot * pad : (slot + 1) * pad] = real
        lhs_ref[band:, slot * pad : (slot + 1) * pad] = imag
        slot += 1

    def put_both(real, imag):
        put(real, imag)
        fill = jnp.zeros((pad - band, pad), f32)
        real_t = jnp.transpose(jnp.concatenate([real, fill], axis=0))[:band]
        imag_t = jnp.transpose(jnp.concatenate([imag, fill], axis=0))[:band]
        put(real_t, -imag_t)

    if stacked:
        every = product(z_ref[...], zc_ref[...])
    depth = max(d for d in range(1, 17) if tiles % d == 0)
    for lag in range(SPAN):

        def part(step):
            left = z_ref[:, pl.ds(lane_tile(LAGS - lag + step * depth), depth * LANES)]
            right = zc_ref[:, pl.ds(lane_tile(step * depth), depth * LANES)]
            return product(left, right)

        if stacked:
            sums = every[2 * band * lag : 2 * band * (lag + 1)]
        else:
            sums = lax.fori_loop(
                0, tiles // depth, lambda step, total: total + part(step), jnp.zeros((2 * band, 2 * pad), f32)
            )
        pair = complex_gram(sums)
        if lag == 0:
            put(*pair)
        else:
            put_both(*pair)

    last = lines - 1
    spot = lax.broadcasted_iota(jnp.int32, (4 * band, LANES), 1) // readout
    top, bottom = spot == 0, spot == last // tiles

    here_top, here_bottom = [
        lax.broadcasted_iota(jnp.int32, (4 * pad, LANES), 1) // readout == group for group in (0, last // tiles)
    ]

    def outer_lines(low_tile, high_tile):
        parts = []
        for tile, where in ((low_tile, top), (high_tile, bottom)):
            start = tile * LANES if stacked else (LAGS + tile) * LANES
            value = [z_ref[at : at + 2 * band, start : start + LANES] for at in (0, 2 * held * band)]
            value = jnp.concatenate(value, axis=0).astype(f32)
            parts.append(jnp.where(where, value, 0.0).astype(jnp.bfloat16))
        right = zc_ref[:, high_tile * LANES : (high_tile + 1) * LANES].astype(f32)
        right = jnp.where(here_bottom, right, 0.0)
        right = jnp.where(here_top, zc_ref[:, low_tile * LANES : (low_tile + 1) * LANES].astype(f32), right)
        return parts[0], parts[1], right.astype(jnp.bfloat16)

    def stack(*lefts):
        rows_of = [left[at : at + 2 * band] for at in (0, 2 * band) for left in lefts]
        return jnp.concatenate(rows_of, axis=0)

    def cut(sums, index):
        return complex_gram(sums[2 * band * index : 2 * band * (index + 1)])

    top_0, bottom_0, right_0 = outer_lines(0, last % tiles)
    top_1, bottom_1, right_1 = outer_lines(1, (last - 1) % tiles)
    with_0 = product(stack(top_0, bottom_0, bottom_1), right_0)
    with_1 = product(stack(top_0, top_1, bottom_1), right_1)
    put(*cut(with_1, 2))
    put(*cut(with_0, 1))
    put(*cut(with_0, 0))
    put(*cut(with_1, 1))
    put_both(*cut(with_0, 2))
    put_both(*cut(with_1, 0))

    high, low = split(lhs_ref[...])
    lead = rhs_ref[:, : 2 * wide]
    total = lax.dot_general(high, lead, NN, preferred_element_type=f32)
    total += lax.dot_general(low, lead, NN, preferred_element_type=f32)
    total += lax.dot_general(high, rhs_ref[:, 2 * wide :], NN, preferred_element_type=f32)
    real = total[:band, :wide] + total[band:, wide:]
    imag = total[:band, wide:] - total[band:, :wide]

    factor = 1.0 / (SPAN**3 * scale)
    column = window % readout
    for part, values in enumerate((real, imag)):
        folded = jnp.zeros((cell, wide), f32)
        for e in range(SPAN):
            moved = values[e * cell : (e + 1) * cell]
            if e != HALF:
                moved = pltpu.roll(moved, (e - HALF) % wide, 1)
            near = column - e + HALF
            folded += jnp.where((near >= 0) & (near < readout), moved, 0.0)
        folded = folded * factor
        for line in range(rows):
            for f in range(frames):
                kept = measured_ref[part, :, line, f, :]
                at = (slice(f * coils, (f + 1) * coils), slice(line * readout, (line + 1) * readout))
                out_ref[part, :, line, f, :] = jnp.where(hit_ref[at] > 0, kept, folded[at])


def pack(lines_ref, estimate_ref, packed_ref, hit_ref):
    _, coils, rows, frames, readout = estimate_ref.shape
    shape = hit_ref.shape
    line = lax.axis_index("slab") * rows + lax.broadcasted_iota(jnp.int32, shape, 1) // readout
    frame = lax.broadcasted_iota(jnp.int32, shape, 0) // coils
    hit = jnp.zeros(shape, jnp.int32)
    for f in range(frames):
        for sample in range(lines_ref.shape[1]):
            hit = jnp.where((line == lines_ref[f, sample]) & (frame == f), 1, hit)
    hit_ref[...] = hit
    groups = LANES // readout
    for part in range(2):
        for f in range(frames):
            for line in range(rows):
                down, right = divmod((part * frames + f) * rows + line, groups)
                at = (0, slice(down * coils, (down + 1) * coils), slice(right * readout, (right + 1) * readout))
                packed_ref[at] = estimate_ref[part, :, line, f, :]
    packed = packed_ref[0]
    for copy in range(1, packed_ref.shape[0]):
        packed_ref[copy] = packed


def gather(copies):
    return lax.all_to_all(copies, "slab", 0, 0)


def stacks(tiles):
    return tiles <= 16


def local(estimate, measured, sampled_lines):
    _, coils, frames, rows, readout = estimate.shape
    slabs = lax.axis_size("slab")
    cell = coils * frames
    width = rows * readout
    band = SPAN * cell
    pad = up(band, LANES)
    wide = up(width, LANES)
    groups = LANES // readout
    tiles = up(slabs * rows, groups) // groups
    reach = up(LAGS, rows) // rows
    slots = 2 * SPAN - 1 + 8
    columns = (tiles if stacks(tiles) else LAGS + tiles) * LANES

    vmem = pl.BlockSpec(memory_space=pltpu.VMEM)
    packed, hit = pl.pallas_call(
        pack,
        out_shape=(
            jax.ShapeDtypeStruct((slabs, up(2 * frames * rows, groups) // groups * coils, LANES), jnp.float32),
            jax.ShapeDtypeStruct((cell, wide), jnp.int32),
        ),
        in_specs=[pl.BlockSpec(memory_space=pltpu.SMEM), vmem],
        out_specs=(vmem, vmem),
        compiler_params=pltpu.CompilerParams(vmem_limit_bytes=56 * 1024 * 1024),
        name="pack",
    )(sampled_lines, jnp.swapaxes(estimate, 2, 3))
    gathered = gather(packed)
    sizes = (slabs, coils, frames, rows, readout)
    result = pl.pallas_call(
        functools.partial(kernel, sizes),
        out_shape=jax.ShapeDtypeStruct((2, coils, rows, frames, readout), jnp.float32),
        in_specs=[vmem, vmem, vmem],
        out_specs=vmem,
        scratch_shapes=[
            pltpu.VMEM((2 * cell, (LAGS + tiles) * LANES), jnp.float32),
            pltpu.VMEM((4 * band * (SPAN if stacks(tiles) else 1), columns), jnp.bfloat16),
            pltpu.VMEM((4 * pad, tiles * LANES), jnp.bfloat16),
            pltpu.VMEM((2 * cell, LANES), jnp.float32),
            pltpu.VMEM((2 * cell, up((2 * reach + 1) * width + LANES, LANES)), jnp.float32),
            pltpu.VMEM((2 * band, slots * pad), jnp.float32),
            pltpu.VMEM((slots * pad, 4 * wide), jnp.bfloat16),
        ],
        compiler_params=pltpu.CompilerParams(vmem_limit_bytes=40 * 1024 * 1024),
        name="filter_step",
    )(hit, gathered, jnp.swapaxes(measured, 2, 3))
    return jnp.swapaxes(result, 2, 3)


def solution(mesh):
    placed = (
        P(None, None, "grp", "slab", None),
        P(None, None, "grp", "slab", None),
        P("grp", None),
    )
    return jax.shard_map(
        local,
        mesh=mesh,
        in_specs=placed,
        out_specs=P(None, None, "grp", "slab", None),
        check_vma=False,
    )
```

time: 24.3 us -> 24.3 us (level)
  no operation moved by 1% of the time
where the time goes in v5:
time: 24.3 us; the launch traced here: 24 us
  blocking collectives  16.5 us (68%)
  Pallas kernels  7.49 us (31%)
    all_to_all x1, blocking collectives, gather(): return lax.all_to_all(copies, 'slab', 0, 0)  16.5 us
    pallas_call x1, Pallas kernels, local(): pl.pallas_call(functools.partial(kernel, sizes), out_shape=jax.ShapeDtype...  5.91 us
    pallas_call x1, Pallas kernels, local(): pl.pallas_call(pack, out_shape=(jax.ShapeDtypeStruct((slabs, up(2 * frame...  1.58 us

profile of v5, /device:TPU:0, one launch (start us, length us, event | category | flops | bytes accessed | tf_op | source)
XLA Modules:
  0.0 24.0 jit_solution(7656993808116553868)
XLA Ops:
  0.0 1.6 %pack.1 = (f32[16,24,128]{2,1,0:T(8,128)}, s32[16,128]{1,0:T(8,128)}) custom-call(s32[2,12]{1,0:T(2,128)} %lines_ref.1, f32[2,8,3,2,32]{4,3,2,1,0:T(2,128)} %bitcast.4), custom_call_target="tpu_custom_call" | custom-call | tf_op jit(solution)/shard_map/pack/pallas_call | solution.py:368
  1.6 0.0 copy-start
  1.6 0.0 copy-start.1
  1.6 16.5 %all_to_all.5.gathered_ref = f32[16,24,128]{2,1,0:T(8,128)S(1)} all-to-all(f32[16,24,128]{2,1,0:T(8,128)} %get-tuple-element.8), channel_id=1, replica_groups=mesh['grp'=2,'slab'=16] {'slab'}, dimensions={0} | all-to-all | bytes 393216 | tf_op jit(solution)/shard_map/all_to_all | solution.py:346
  18.1 0.0 copy-done
  18.1 0.0 copy-done.1
  18.1 5.9 %filter_step.1 = f32[2,8,3,2,32]{4,3,2,1,0:T(2,128)} custom-call(s32[16,128]{1,0:T(8,128)S(1)} %copy-done.1, f32[16,24,128]{2,1,0:T(8,128)S(1)} %all_to_all.5.gathered_ref, f32[2,8,3,2,32]{4,3,2,1,0:T(2,128)S(1)} %bitcast.3), custom_call_target="tpu_custom_call" | custom-call | tf_op jit(solution)/shard_map/filter_step/pallas_call | solution.py:381
Async XLA Ops:
  1.6 16.5 %copy-start = (f32[2,8,2,3,32]{4,2,3,1,0:T(2,128)S(1)}, f32[2,8,2,3,32]{4,2,3,1,0:T(2,128)}, u32[]{:S(2)}) copy-start(f32[2,8,2,3,32]{4,2,3,1,0:T(2,128)} %param.4) | copy-start | bytes 36868
  1.6 16.5 %copy-start.1 = (s32[16,128]{1,0:T(8,128)S(1)}, s32[16,128]{1,0:T(8,128)}, u32[]{:S(2)}) copy-start(s32[16,128]{1,0:T(8,128)} %get-tuple-element.7.hit_ref) | copy-start | bytes 24580

commit v6 on v4

--- a/solution.py
+++ b/solution.py
@@ -37,7 +37,7 @@
     return start if isinstance(start, int) else pl.multiple_of(start, LANES)
 
 
-def kernel(sizes, hit_ref, gathered_ref, measured_ref, out_ref, x_ref, z_ref, zc_ref, acc_ref, xw_ref, lhs_ref, rhs_ref):
+def kernel(sizes, hit_ref, gathered_ref, measured_ref, result_ref, x_ref, z_ref, zc_ref, acc_ref, xw_ref, lhs_ref, rhs_ref, out_ref, sems):
     slabs, coils, frames, rows, readout = sizes
     me = lax.axis_index("slab")
     cell = coils * frames
@@ -283,6 +283,7 @@
 
     factor = 1.0 / (SPAN**3 * scale)
     column = window % readout
+    leaving = []
     for part, values in enumerate((real, imag)):
         folded = jnp.zeros((cell, wide), f32)
         for e in range(SPAN):
@@ -297,19 +298,20 @@
                 kept = measured_ref[part, :, line, f, :]
                 at = (slice(f * coils, (f + 1) * coils), slice(line * readout, (line + 1) * readout))
                 out_ref[part, :, line, f, :] = jnp.where(hit_ref[at] > 0, kept, folded[at])
-
-
-def pack(lines_ref, estimate_ref, packed_ref, hit_ref):
+        leaving.append(pltpu.make_async_copy(out_ref.at[part], result_ref.at[part], sems.at[part]))
+        leaving[part].start()
+    for copy in leaving:
+        copy.wait()
+
+
+def pack(table_ref, source_ref, blocks_ref, mask_ref, lines_ref, estimate_ref, packed_ref, hit_ref, sems):
+    coming = pltpu.make_async_copy(source_ref, estimate_ref, sems.at[0])
+    coming.start()
+    table = pltpu.make_async_copy(table_ref, lines_ref, sems.at[1])
+    table.start()
     _, coils, rows, frames, readout = estimate_ref.shape
-    shape = hit_ref.shape
-    line = lax.axis_index("slab") * rows + lax.broadcasted_iota(jnp.int32, shape, 1) // readout
-    frame = lax.broadcasted_iota(jnp.int32, shape, 0) // coils
-    hit = jnp.zeros(shape, jnp.int32)
-    for f in range(frames):
-        for sample in range(lines_ref.shape[1]):
-            hit = jnp.where((line == lines_ref[f, sample]) & (frame == f), 1, hit)
-    hit_ref[...] = hit
     groups = LANES // readout
+    coming.wait()
     for part in range(2):
         for f in range(frames):
             for line in range(rows):
@@ -319,6 +321,21 @@
     packed = packed_ref[0]
     for copy in range(1, packed_ref.shape[0]):
         packed_ref[copy] = packed
+    leaving = pltpu.make_async_copy(packed_ref, blocks_ref, sems.at[2])
+    leaving.start()
+    table.wait()
+    shape = hit_ref.shape
+    line = lax.axis_index("slab") * rows + lax.broadcasted_iota(jnp.int32, shape, 1) // readout
+    frame = lax.broadcasted_iota(jnp.int32, shape, 0) // coils
+    hit = jnp.zeros(shape, jnp.int32)
+    for f in range(frames):
+        for sample in range(lines_ref.shape[1]):
+            hit = jnp.where((line == lines_ref[f, sample]) & (frame == f), 1, hit)
+    hit_ref[...] = hit
+    marking = pltpu.make_async_copy(hit_ref, mask_ref, sems.at[3])
+    marking.start()
+    leaving.wait()
+    marking.wait()
 
 
 def gather(copies):
@@ -344,14 +361,20 @@
     columns = (tiles if stacks(tiles) else LAGS + tiles) * LANES
 
     vmem = pl.BlockSpec(memory_space=pltpu.VMEM)
+    blocks = (slabs, up(2 * frames * rows, groups) // groups * coils, LANES)
+    hbm = pl.BlockSpec(memory_space=pl.ANY)
     packed, hit = pl.pallas_call(
         pack,
-        out_shape=(
-            jax.ShapeDtypeStruct((slabs, up(2 * frames * rows, groups) // groups * coils, LANES), jnp.float32),
-            jax.ShapeDtypeStruct((cell, wide), jnp.int32),
-        ),
-        in_specs=[pl.BlockSpec(memory_space=pltpu.SMEM), vmem],
-        out_specs=(vmem, vmem),
+        out_shape=(jax.ShapeDtypeStruct(blocks, jnp.float32), jax.ShapeDtypeStruct((cell, wide), jnp.int32)),
+        in_specs=[hbm, hbm],
+        out_specs=(hbm, hbm),
+        scratch_shapes=[
+            pltpu.SMEM(sampled_lines.shape, jnp.int32),
+            pltpu.VMEM((2, coils, rows, frames, readout), jnp.float32),
+            pltpu.VMEM(blocks, jnp.float32),
+            pltpu.VMEM((cell, wide), jnp.int32),
+            pltpu.SemaphoreType.DMA((4,)),
+        ],
         compiler_params=pltpu.CompilerParams(vmem_limit_bytes=56 * 1024 * 1024),
         name="pack",
     )(sampled_lines, jnp.swapaxes(estimate, 2, 3))
@@ -361,7 +384,7 @@
         functools.partial(kernel, sizes),
         out_shape=jax.ShapeDtypeStruct((2, coils, rows, frames, readout), jnp.float32),
         in_specs=[vmem, vmem, vmem],
-        out_specs=vmem,
+        out_specs=hbm,
         scratch_shapes=[
             pltpu.VMEM((2 * cell, (LAGS + tiles) * LANES), jnp.float32),
             pltpu.VMEM((4 * band * (SPAN if stacks(tiles) else 1), columns), jnp.bfloat16),
@@ -370,6 +393,8 @@
             pltpu.VMEM((2 * cell, up((2 * reach + 1) * width + LANES, LANES)), jnp.float32),
             pltpu.VMEM((2 * band, slots * pad), jnp.float32),
             pltpu.VMEM((slots * pad, 4 * wide), jnp.bfloat16),
+            pltpu.VMEM((2, coils, rows, frames, readout), jnp.float32),
+            pltpu.SemaphoreType.DMA((2,)),
         ],
         compiler_params=pltpu.CompilerParams(vmem_limit_bytes=40 * 1024 * 1024),
         name="filter_step",

time: 24.3 us -> 24.4 us (level)
  no operation moved by 1% of the time
where the time goes in v6:
time: 24.4 us; the launch traced here: 24.1 us
  blocking collectives  16.5 us (68%)
  Pallas kernels  7.53 us (31%)
    all_to_all x1, blocking collectives, gather(): return lax.all_to_all(copies, 'slab', 0, 0)  16.5 us
    pallas_call x1, Pallas kernels, local(): pl.pallas_call(functools.partial(kernel, sizes), out_shape=jax.ShapeDtype...  5.92 us
    pallas_call x1, Pallas kernels, local(): pl.pallas_call(pack, out_shape=(jax.ShapeDtypeStruct(blocks, jnp.float32)...  1.6 us

profile of v6, /device:TPU:0, one launch (start us, length us, event | category | flops | bytes accessed | tf_op | source)
XLA Modules:
  0.0 24.1 jit_solution(989459302698950450)
XLA Ops:
  0.0 1.6 %pack.1 = (f32[16,24,128]{2,1,0:T(8,128)}, s32[16,128]{1,0:T(8,128)}) custom-call(s32[2,12]{1,0:T(2,128)} %table_ref.1, f32[2,8,3,2,32]{4,3,2,1,0:T(2,128)} %bitcast.4), custom_call_target="tpu_custom_call" | custom-call | tf_op jit(solution)/shard_map/pack/pallas_call | solution.py:366
  1.6 0.0 copy-start
  1.6 0.0 copy-start.1
  1.6 16.5 %all_to_all.5.gathered_ref = f32[16,24,128]{2,1,0:T(8,128)S(1)} all-to-all(f32[16,24,128]{2,1,0:T(8,128)} %get-tuple-element.8), channel_id=1, replica_groups=mesh['grp'=2,'slab'=16] {'slab'}, dimensions={0} | all-to-all | bytes 393216 | tf_op jit(solution)/shard_map/all_to_all | solution.py:342
  18.2 0.0 copy-done
  18.2 0.0 copy-done.1
  18.2 5.9 %filter_step.1 = f32[2,8,3,2,32]{4,3,2,1,0:T(2,128)} custom-call(s32[16,128]{1,0:T(8,128)S(1)} %copy-done.1, f32[16,24,128]{2,1,0:T(8,128)S(1)} %all_to_all.5.gathered_ref, f32[2,8,3,2,32]{4,3,2,1,0:T(2,128)S(1)} %bitcast.3), custom_call_target="tpu_custom_call" | custom-call | tf_op jit(solution)/shard_map/filter_step/pallas_call | solution.py:383
Async XLA Ops:
  1.6 16.5 %copy-start = (f32[2,8,2,3,32]{4,2,3,1,0:T(2,128)S(1)}, f32[2,8,2,3,32]{4,2,3,1,0:T(2,128)}, u32[]{:S(2)}) copy-start(f32[2,8,2,3,32]{4,2,3,1,0:T(2,128)} %param.4) | copy-start | bytes 36868
  1.6 16.5 %copy-start.1 = (s32[16,128]{1,0:T(8,128)S(1)}, s32[16,128]{1,0:T(8,128)}, u32[]{:S(2)}) copy-start(s32[16,128]{1,0:T(8,128)} %get-tuple-element.7.hit_ref) | copy-start | bytes 24580

commit v7 on v4

--- a/solution.py
+++ b/solution.py
@@ -53,7 +53,7 @@
 
     def unpacked(block, plane, line):
         down, right = divmod(plane * rows + line, groups)
-        return gathered_ref[block, down * coils : (down + 1) * coils, right * readout : (right + 1) * readout]
+        return gathered_ref[place(block, slabs), down * coils : (down + 1) * coils, right * readout : (right + 1) * readout]
 
     if tiles * groups != lines:
         x_ref[...] = jnp.zeros_like(x_ref)
@@ -321,8 +321,25 @@
         packed_ref[copy] = packed
 
 
-def gather(copies):
-    return lax.all_to_all(copies, "slab", 0, 0)
+def steps(slabs):
+    return [(slabs // 4, 4), (2, 2), (2, 1)] if slabs % 4 == 0 else [(slabs, 1)]
+
+
+def place(block, slabs):
+    spot, weight = 0, 1
+    for size, stride in steps(slabs):
+        spot += block // stride % size * weight
+        weight *= size
+    return spot
+
+
+def gather(held):
+    slabs = lax.axis_size("slab")
+    for size, stride in steps(slabs):
+        firsts = [i for i in range(slabs) if i // stride % size == 0]
+        groups = [[i + j * stride for j in range(size)] for i in firsts]
+        held = lax.all_gather(held, "slab", axis_index_groups=groups, tiled=True)
+    return held
 
 
 def stacks(tiles):
@@ -347,7 +364,7 @@
     packed, hit = pl.pallas_call(
         pack,
         out_shape=(
-            jax.ShapeDtypeStruct((slabs, up(2 * frames * rows, groups) // groups * coils, LANES), jnp.float32),
+            jax.ShapeDtypeStruct((1, up(2 * frames * rows, groups) // groups * coils, LANES), jnp.float32),
             jax.ShapeDtypeStruct((cell, wide), jnp.int32),
         ),
         in_specs=[pl.BlockSpec(memory_space=pltpu.SMEM), vmem],

time: 24.3 us -> 29.4 us (1.21)
  blocking collectives: 16.5 us -> 21.8 us
    all_gather x0 -> x3, blocking collectives: none -> 21.8 us  [gather(): held = lax.all_gather(held, 'slab', axis_index_groups=groups, tiled=True)]
    all_to_all x1 -> x0, blocking collectives: 16.5 us -> none  [gather(): return lax.all_to_all(copies, 'slab', 0, 0)]
where the time goes in v7:
time: 29.4 us; the launch traced here: 29.2 us
  blocking collectives  21.8 us (74%)
  Pallas kernels  7.41 us (25%)
    all_gather x3, blocking collectives, gather(): held = lax.all_gather(held, 'slab', axis_index_groups=groups, tiled=True)  21.8 us
    pallas_call x1, Pallas kernels, local(): pl.pallas_call(functools.partial(kernel, sizes), out_shape=jax.ShapeDtype...  5.91 us
    pallas_call x1, Pallas kernels, local(): pl.pallas_call(pack, out_shape=(jax.ShapeDtypeStruct((1, up(2 * frames *...  1.5 us

profile of v7, /device:TPU:0, one launch (start us, length us, event | category | flops | bytes accessed | tf_op | source)
XLA Modules:
  0.0 29.2 jit_solution(3965750805721339220)
XLA Ops:
  0.0 1.5 %pack.1 = (f32[1,24,128]{2,1,0:T(8,128)}, s32[16,128]{1,0:T(8,128)}) custom-call(s32[2,12]{1,0:T(2,128)} %lines_ref.1, f32[2,8,3,2,32]{4,3,2,1,0:T(2,128)} %bitcast.4), custom_call_target="tpu_custom_call" | custom-call | tf_op jit(solution)/shard_map/pack/pallas_call | solution.py:364
  1.5 14.9 %all_gather.9 = f32[4,24,128]{2,1,0:T(8,128)S(1)} all-gather(f32[1,24,128]{2,1,0:T(8,128)} %get-tuple-element.8), channel_id=1, replica_groups={{0,4,8,12},{1,5,9,13},{2,6,10,14},{3,7,11,15},{16,20,24,28},{17,21,25,2..., dimensions={0}, use_global_device_ids=true | all-gather | bytes 61440 | tf_op jit(solution)/shard_map/all_gather | solution.py:341
  16.4 4.8 %all_gather.10 = f32[8,24,128]{2,1,0:T(8,128)S(1)} all-gather(f32[4,24,128]{2,1,0:T(8,128)S(1)} %all_gather.9), channel_id=1, replica_groups={{0,2},{1,3},{4,6},{5,7},{8,10},{9,11},{12,14},{13,15},{16,18},{17,19},{..., dimensions={0}, use_global_device_ids=true | all-gather | bytes 147456 | tf_op jit(solution)/shard_map/all_gather | solution.py:341
  21.2 0.0 copy-start
  21.2 0.0 copy-start.1
  21.2 2.1 %all_gather.11.gathered_ref = f32[16,24,128]{2,1,0:T(8,128)S(1)} all-gather(f32[8,24,128]{2,1,0:T(8,128)S(1)} %all_gather.10), channel_id=1, replica_groups={{0,1},{2,3},{4,5},{6,7},{8,9},{10,11},{12,13},{14,15},{16,17},{18,19},{..., dimensions={0}, use_global_device_ids=true | all-gather | bytes 294912 | tf_op jit(solution)/shard_map/all_gather | solution.py:341
  23.3 0.0 copy-done
  23.3 0.0 copy-done.1
  23.3 5.9 %filter_step.1 = f32[2,8,3,2,32]{4,3,2,1,0:T(2,128)} custom-call(s32[16,128]{1,0:T(8,128)S(1)} %copy-done.1, f32[16,24,128]{2,1,0:T(8,128)S(1)} %all_gather.11.gathered_ref, f32[2,8,3,2,32]{4,3,2,1,0:T(2,128)S(1)} %bitcast.3), custom_call_target="tpu_custom_call" | custom-call | tf_op jit(solution)/shard_map/filter_step/pallas_call | solution.py:377
Async XLA Ops:
  21.2 2.1 %copy-start = (f32[2,8,2,3,32]{4,2,3,1,0:T(2,128)S(1)}, f32[2,8,2,3,32]{4,2,3,1,0:T(2,128)}, u32[]{:S(2)}) copy-start(f32[2,8,2,3,32]{4,2,3,1,0:T(2,128)} %param.4) | copy-start | bytes 36868
  21.2 2.1 %copy-start.1 = (s32[16,128]{1,0:T(8,128)S(1)}, s32[16,128]{1,0:T(8,128)}, u32[]{:S(2)}) copy-start(s32[16,128]{1,0:T(8,128)} %get-tuple-element.7.hit_ref) | copy-start | bytes 24580

commit v8 on v4

--- a/solution.py
+++ b/solution.py
@@ -53,7 +53,7 @@
 
     def unpacked(block, plane, line):
         down, right = divmod(plane * rows + line, groups)
-        return gathered_ref[block, down * coils : (down + 1) * coils, right * readout : (right + 1) * readout]
+        return gathered_ref[place(block, slabs), down * coils : (down + 1) * coils, right * readout : (right + 1) * readout]
 
     if tiles * groups != lines:
         x_ref[...] = jnp.zeros_like(x_ref)
@@ -321,8 +321,21 @@
         packed_ref[copy] = packed
 
 
-def gather(copies):
-    return lax.all_to_all(copies, "slab", 0, 0)
+def nearby(slabs):
+    return 2 if slabs % 2 == 0 else 1
+
+
+def place(block, slabs):
+    near = nearby(slabs)
+    return block % near * (slabs // near) + block // near
+
+
+def gather(copies, slabs):
+    near, far = nearby(slabs), slabs // nearby(slabs)
+    alike = [[i + j * near for j in range(far)] for i in range(near)]
+    chips = [[i * near + j for j in range(near)] for i in range(far)]
+    half = lax.all_to_all(copies, "slab", 0, 0, axis_index_groups=alike)
+    return lax.all_gather(half, "slab", axis_index_groups=chips, tiled=True)
 
 
 def stacks(tiles):
@@ -347,7 +360,7 @@
     packed, hit = pl.pallas_call(
         pack,
         out_shape=(
-            jax.ShapeDtypeStruct((slabs, up(2 * frames * rows, groups) // groups * coils, LANES), jnp.float32),
+            jax.ShapeDtypeStruct((slabs // nearby(slabs), up(2 * frames * rows, groups) // groups * coils, LANES), jnp.float32),
             jax.ShapeDtypeStruct((cell, wide), jnp.int32),
         ),
         in_specs=[pl.BlockSpec(memory_space=pltpu.SMEM), vmem],
@@ -355,7 +368,7 @@
         compiler_params=pltpu.CompilerParams(vmem_limit_bytes=56 * 1024 * 1024),
         name="pack",
     )(sampled_lines, jnp.swapaxes(estimate, 2, 3))
-    gathered = gather(packed)
+    gathered = gather(packed, slabs)
     sizes = (slabs, coils, frames, rows, readout)
     result = pl.pallas_call(
         functools.partial(kernel, sizes),

time: 24.3 us -> 24.2 us (level)
    all_to_all x1, blocking collectives: 16.5 us -> 14.4 us  [gather(): half = lax.all_to_all(copies, 'slab', 0, 0, axis_index_groups=alike)]
    all_gather x0 -> x1, blocking collectives: none -> 2.07 us  [gather(): return lax.all_gather(half, 'slab', axis_index_groups=chips, tiled=True)]
where the time goes in v8:
time: 24.2 us; the launch traced here: 23.9 us
  blocking collectives  16.5 us (68%)
  Pallas kernels  7.43 us (31%)
    all_to_all x1, blocking collectives, gather(): half = lax.all_to_all(copies, 'slab', 0, 0, axis_index_groups=alike)  14.4 us
    pallas_call x1, Pallas kernels, local(): pl.pallas_call(functools.partial(kernel, sizes), out_shape=jax.ShapeDtype...  5.9 us
    all_gather x1, blocking collectives, gather(): return lax.all_gather(half, 'slab', axis_index_groups=chips, tiled=True)  2.07 us
    pallas_call x1, Pallas kernels, local(): pl.pallas_call(pack, out_shape=(jax.ShapeDtypeStruct((slabs // nearby(sla...  1.54 us

profile of v8, /device:TPU:0, one launch (start us, length us, event | category | flops | bytes accessed | tf_op | source)
XLA Modules:
  0.0 23.9 jit_solution(169925431043993206)
XLA Ops:
  0.0 1.5 %pack.1 = (f32[8,24,128]{2,1,0:T(8,128)}, s32[16,128]{1,0:T(8,128)}) custom-call(s32[2,12]{1,0:T(2,128)} %lines_ref.1, f32[2,8,3,2,32]{4,3,2,1,0:T(2,128)} %bitcast.4), custom_call_target="tpu_custom_call" | custom-call | tf_op jit(solution)/shard_map/pack/pallas_call | solution.py:360
  1.5 14.4 %all_to_all.5 = f32[8,24,128]{2,1,0:T(8,128)S(1)} all-to-all(f32[8,24,128]{2,1,0:T(8,128)} %get-tuple-element.8), channel_id=1, replica_groups={{0,2,4,6,8,10,12,14},{1,3,5,7,9,11,13,15},{16,18,20,22,24,26,28,30},{17..., dimensions={0} | all-to-all | bytes 196608 | tf_op jit(solution)/shard_map/all_to_all | solution.py:337
  15.9 0.0 copy-start
  15.9 0.0 copy-start.1
  15.9 2.1 %all_gather.3.gathered_ref = f32[16,24,128]{2,1,0:T(8,128)S(1)} all-gather(f32[8,24,128]{2,1,0:T(8,128)S(1)} %all_to_all.5), channel_id=1, replica_groups={{0,1},{2,3},{4,5},{6,7},{8,9},{10,11},{12,13},{14,15},{16,17},{18,19},{..., dimensions={0}, use_global_device_ids=true | all-gather | bytes 294912 | tf_op jit(solution)/shard_map/all_gather | solution.py:338
  18.0 0.0 copy-done
  18.0 0.0 copy-done.1
  18.0 5.9 %filter_step.1 = f32[2,8,3,2,32]{4,3,2,1,0:T(2,128)} custom-call(s32[16,128]{1,0:T(8,128)S(1)} %copy-done.1, f32[16,24,128]{2,1,0:T(8,128)S(1)} %all_gather.3.gathered_ref, f32[2,8,3,2,32]{4,3,2,1,0:T(2,128)S(1)} %bitcast.3), custom_call_target="tpu_custom_call" | custom-call | tf_op jit(solution)/shard_map/filter_step/pallas_call | solution.py:373
Async XLA Ops:
  15.9 2.1 %copy-start = (f32[2,8,2,3,32]{4,2,3,1,0:T(2,128)S(1)}, f32[2,8,2,3,32]{4,2,3,1,0:T(2,128)}, u32[]{:S(2)}) copy-start(f32[2,8,2,3,32]{4,2,3,1,0:T(2,128)} %param.4) | copy-start | bytes 36868
  15.9 2.1 %copy-start.1 = (s32[16,128]{1,0:T(8,128)S(1)}, s32[16,128]{1,0:T(8,128)}, u32[]{:S(2)}) copy-start(s32[16,128]{1,0:T(8,128)} %get-tuple-element.7.hit_ref) | copy-start | bytes 24580
